TPU v7x, 32 devices: a whole 2x2x4 slice. The times are simulated.
32 devices in a mesh: groups: 2 (over x), seq: 4 (over z), expert: 4 (over y, core).
Axes of the slice: x: 2, y: 2, z: 4, core: 2. Of those that a mesh axis runs over, the one named last changes fastest.
Arguments:
- q_lat: bfloat16 [512, 65536], P(('groups', 'seq'), 'expert'), parts along dimension 0, may hold values from -36 to 36
- q_rope: bfloat16 [512, 8192], P(('groups', 'seq'), 'expert'), parts along dimension 0, may hold values from -6 to 6
- cache_lat: bfloat16 [2048, 512], P(('groups', 'seq')), parts along dimension 0, may hold values from -7 to 7
- cache_rope: bfloat16 [2048, 64], P(('groups', 'seq')), parts along dimension 0, may hold values from -8 to 8
- tool_lat: bfloat16 [256, 512], P(('groups', 'seq')), parts along dimension 0, may hold values from -2.5 to 2.5
- tool_rope: bfloat16 [256, 64], P(('groups', 'seq')), parts along dimension 0, may hold values from -8 to 8
- offset: int32 [2], P('groups'), parts along dimension 0, may hold values from 512 to 736
- suf_lat: bfloat16 [512, 512], P(('groups', 'seq')), parts along dimension 0, may hold values from -6 to 6
- suf_rope: bfloat16 [512, 64], P(('groups', 'seq')), parts along dimension 0, may hold values from -8 to 8
- w_uv: bfloat16 [128, 512, 128], P('expert'), may hold values from -1 to 1
- w_out: bfloat16 [16384, 7168], P('expert', 'seq'), may hold values from -0.19921875 to 0.19921875
- resid: bfloat16 [512, 7168], P(('groups', 'expert'), 'seq'), parts along dimension 0, may hold values from -36 to 36
- routes: int32 [512, 2], P(('groups', 'expert')), parts along dimension 0, may hold values from 0 to 3, all different within a row; in each aligned block of 64 rows (0 to 63, 64 to 127, ...) at most 40 rows name the same one
- probs: float32 [512, 2], P(('groups', 'expert')), parts along dimension 0, may hold values from 0.1 to 1
- w_gate: bfloat16 [4, 7168, 1024], P('expert', None, 'seq'), may hold values from -0.0625 to 0.0625
- w_up: bfloat16 [4, 7168, 1024], P('expert', None, 'seq'), may hold values from -0.0625 to 0.0625
- w_down: bfloat16 [4, 1024, 7168], P('expert', 'seq'), may hold values from -0.1875 to 0.1875
Outputs:
- attn_residual: bfloat16 [512, 7168], P(('groups', 'expert'), 'seq'), parts along dimension 0
- expert_mix: bfloat16 [512, 7168], P(('groups', 'expert'), 'seq'), parts along dimension 0
There are 2 independent parts, one for each index of `groups`. A program takes and returns all parts, laid end to end along the dimension named above; an argument that names none is the same for every part. Nothing has to cross between parts.
Inputs may be any that keep to these rules, and one draw needn't show every extreme that they name: `routes`: within the rows of one device of the expert axis (64 rows in a row), no expert is named more than 40 times.
All inputs are finite; a program needn't handle non-finite values.
Results may differ from a plain program's by a relative error of at most 0.03.
Values may be sent and summed in bfloat16 or wider, within the bound.
A program may use at most 128 MiB of HBM per device.

v0:
```python
import jax
import jax.numpy as jnp
from jax import lax
from jax.sharding import PartitionSpec as P

score_scale = 192.0 ** (-0.5)
floor_score = -1e30
norm_eps = 1e-06


def run_expert(tokens_in, w_gate, w_up, w_down):
    sources, count, width = tokens_in.shape
    rows = tokens_in.reshape(sources * count, width)
    gate = jnp.dot(rows, w_gate[0], preferred_element_type=jnp.float32)
    upper = jnp.dot(rows, w_up[0], preferred_element_type=jnp.float32)
    inner = (jax.nn.silu(gate) * upper).astype(jnp.bfloat16)
    partial_out = jnp.dot(inner, w_down[0], preferred_element_type=jnp.float32).reshape(
        sources, count, width
    )
    summed = lax.psum_scatter(
        partial_out.astype(jnp.bfloat16), "seq", scatter_dimension=2, tiled=True
    )
    return lax.all_to_all(summed, "expert", split_axis=0, concat_axis=0, tiled=True)


def on_device(
    q_lat,
    q_rope,
    cache_lat,
    cache_rope,
    tool_lat,
    tool_rope,
    offset,
    suf_lat,
    suf_rope,
    w_uv,
    w_out,
    resid,
    routes,
    probs,
    w_gate,
    w_up,
    w_down,
):
    seq_index = lax.axis_index("seq")
    ctx_dev = cache_lat.shape[0]
    query_dev = q_lat.shape[0]
    heads_dev, lat_width, value_width = w_uv.shape
    rope_width = cache_rope.shape[1]
    tool_all_lat, tool_all_rope = (
        lax.all_gather(tool_lat, "seq", axis=0, tiled=True),
        lax.all_gather(tool_rope, "seq", axis=0, tiled=True),
    )
    tool_len = tool_all_lat.shape[0]
    position = seq_index * ctx_dev + jnp.arange(ctx_dev, dtype=jnp.int32)
    shifted = position - offset[0]
    inside = (shifted >= 0) & (shifted < tool_len)
    safe = jnp.clip(shifted, 0, tool_len - 1)
    ctx_lat = jnp.where(inside[:, None], jnp.take(tool_all_lat, safe, axis=0), cache_lat)
    ctx_rope = jnp.where(inside[:, None], jnp.take(tool_all_rope, safe, axis=0), cache_rope)
    local_lat = jnp.concatenate([ctx_lat, suf_lat], axis=0)
    local_rope = jnp.concatenate([ctx_rope, suf_rope], axis=0)
    block_len = ctx_dev + query_dev
    query_rows = query_dev * heads_dev
    queries_lat = q_lat.reshape(query_rows, lat_width)
    queries_rope = q_rope.reshape(query_rows, rope_width)
    query_pos = seq_index * query_dev + jnp.arange(query_rows, dtype=jnp.int32) // heads_dev
    running_max = jnp.full((query_rows,), floor_score, jnp.float32)
    piece_lat = lax.all_gather(local_lat, "seq", axis=0, tiled=True)
    piece_rope = lax.all_gather(local_rope, "seq", axis=0, tiled=True)
    global_row = jnp.arange(piece_lat.shape[0], dtype=jnp.int32)
    within = global_row % block_len
    owner = global_row // block_len
    is_context = within < ctx_dev
    suffix_pos = owner * query_dev + within - ctx_dev
    visible = is_context[None, :] | (suffix_pos[None, :] <= query_pos[:, None])
    scores = jnp.einsum("qc,kc->qk", queries_lat, piece_lat, preferred_element_type=jnp.float32)
    scores = (
        scores
        + jnp.einsum("qc,kc->qk", queries_rope, piece_rope, preferred_element_type=jnp.float32)
    ) * score_scale
    scores = jnp.where(visible, scores, floor_score)
    new_max = jnp.maximum(running_max, jnp.max(scores, axis=1))
    weights = jnp.where(visible, jnp.exp(scores - new_max[:, None]), 0.0)
    new_total = jnp.sum(weights, axis=1)
    new_acc = jnp.dot(weights.astype(jnp.bfloat16), piece_lat, preferred_element_type=jnp.float32)
    latent_out = (
        (new_acc / new_total[:, None]).astype(jnp.bfloat16).reshape(query_dev, heads_dev, lat_width)
    )
    head_vals = jnp.einsum(
        "thc,hcv->thv", latent_out, w_uv, preferred_element_type=jnp.float32
    ).astype(jnp.bfloat16)
    head_vals = head_vals.reshape(query_dev, heads_dev * value_width)
    all_values = lax.all_gather(head_vals, "seq", axis=0, tiled=True)
    tok_dev = resid.shape[0]
    attn_sum = lax.psum_scatter(
        jnp.dot(all_values, w_out, preferred_element_type=jnp.float32).astype(jnp.bfloat16),
        "expert",
        scatter_dimension=0,
        tiled=True,
    ).astype(jnp.float32)
    attn_residual = (resid.astype(jnp.float32) + attn_sum).astype(jnp.bfloat16)
    expert_count = lax.axis_size("expert") * w_gate.shape[0]
    top_count = routes.shape[1]
    capacity = tok_dev * top_count * 5 // (4 * expert_count)
    flat_routes = routes.reshape(-1)
    one_hot = (flat_routes[:, None] == jnp.arange(expert_count, dtype=jnp.int32)[None, :]).astype(
        jnp.int32
    )
    earlier = jnp.cumsum(one_hot, axis=0) - one_hot
    slot = jnp.sum(earlier * one_hot, axis=1)
    target = (flat_routes * capacity + slot).reshape(tok_dev, top_count)
    slot_ids = jnp.arange(expert_count * capacity, dtype=jnp.int32)
    matches = slot_ids[:, None, None] == target[None, :, :]
    send_matrix = jnp.any(matches, axis=2).astype(jnp.bfloat16)
    route_weight = 2.5 * probs / jnp.sum(probs, axis=1, keepdims=True)
    gather_matrix = jnp.sum(jnp.where(matches, route_weight[None, :, :], 0.0), axis=2).T
    whole_stream = lax.all_gather(attn_residual, "seq", axis=1, tiled=True).astype(jnp.float32)
    normed = (
        whole_stream
        * lax.rsqrt(jnp.mean(whole_stream * whole_stream, axis=1, keepdims=True) + norm_eps)
    ).astype(jnp.bfloat16)
    outgoing = jnp.dot(send_matrix, normed, preferred_element_type=jnp.float32).astype(jnp.bfloat16)
    outgoing = outgoing.reshape(expert_count, capacity, normed.shape[1])
    returned = run_expert(
        lax.all_to_all(outgoing, "expert", split_axis=0, concat_axis=0, tiled=True),
        w_gate,
        w_up,
        w_down,
    )
    returned = returned.reshape(expert_count * capacity, returned.shape[2]).astype(jnp.float32)
    expert_mix = jnp.dot(
        gather_matrix, returned, precision=lax.Precision.HIGHEST, preferred_element_type=jnp.float32
    )
    return (attn_residual, expert_mix.astype(jnp.bfloat16))


def solution(mesh):
    placed = (
        P(("groups", "seq"), "expert"),
        P(("groups", "seq"), "expert"),
        P(("groups", "seq"), None),
        P(("groups", "seq"), None),
        P(("groups", "seq"), None),
        P(("groups", "seq"), None),
        P("groups"),
        P(("groups", "seq"), None),
        P(("groups", "seq"), None),
        P("expert", None, None),
        P("expert", "seq"),
        P(("groups", "expert"), "seq"),
        P(("groups", "expert"), None),
        P(("groups", "expert"), None),
        P("expert", None, "seq"),
        P("expert", None, "seq"),
        P("expert", "seq", None),
    )
    return jax.shard_map(
        on_device,
        mesh=mesh,
        in_specs=placed,
        out_specs=(P(("groups", "expert"), "seq"), P(("groups", "expert"), "seq")),
        check_vma=False,
    )
```

profile of v0, /device:TPU:0, one launch (start us, length us, event | category | flops | bytes accessed | tf_op | source)
XLA Modules:
  0.0 290.7 jit_solution(17597389861939251030)
XLA Ops:
  7.2 0.0 all-gather.4.cloned.1.call-start
  8.1 15.3 %all_gather.18 = bf16[128,512]{1,0:T(8,128)(2,1)S(1)} all-gather(bf16[32,512]{1,0:T(8,128)(2,1)} %param.21), channel_id=1, replica_groups=mesh['groups'=2,'seq'=4,'expert'=4] {'seq'}, dimensions={0}, use_global_device_ids=true | all-gather | bytes 163840 | tf_op jit(solution)/shard_map/all_gather | solution.py:51
  23.3 1.2 gather_fusion
  24.5 0.0 copy-start.6
  24.5 0.0 copy-start.7
  24.5 1.1 select_select_fusion
  25.6 0.0 copy-start.4
  25.6 1.6 pad_maximum_fusion
  27.3 0.0 all-gather.4.cloned.1.call-update
  27.3 0.0 all-gather.6.cloned.1.call-start
  27.3 2.4 reshape.119
  29.7 13.2 %all_gather.20 = bf16[128,64]{1,0:T(8,128)(2,1)S(1)} all-gather(bf16[32,64]{1,0:T(8,128)(2,1)S(1)} %copy-done.8), channel_id=1, replica_groups=mesh['groups'=2,'seq'=4,'expert'=4] {'seq'}, dimensions={0}, use_global_device_ids=true | all-gather | bytes 20480 | tf_op jit(solution)/shard_map/all_gather | solution.py:52
  42.9 0.9 gather_fusion.1
  43.8 0.1 copy.58
  43.9 0.1 select_select_fusion.1
  44.1 0.1 copy.59
  44.2 15.2 %all-gather = bf16[4,320,64]{1,2,0:T(8,128)(2,1)S(1)} all-gather(bf16[1,320,64]{1,2,0:T(8,128)(2,1)S(1)} %copy.59), channel_id=1, replica_groups=mesh['groups'=2,'seq'=4,'expert'=4] {'seq'}, dimensions={0}, use_global_device_ids=true | all-gather | bytes 204800 | tf_op jit(solution)/shard_map/all_gather | solution.py:70
  59.3 0.2 copy.60
  59.5 0.2 reshape.143
  59.7 0.5 reshape.120
  60.2 3.9 %all-gather.4.cloned.1.call-done = bf16[1280,512]{1,0:T(8,128)(2,1)} async-done(((bf16[320,512]{1,0:T(8,128)(2,1)}), bf16[1280,512]{1,0:T(8,128)(2,1)}) %all-gather.4.cloned.1.call-update) | async-done | bytes 1310736 | tf_op jit(solution)/shard_map/all_gather | solution.py:69
  64.1 5.0 %fusion.51 = f32[1280,2048]{1,0:T(8,128)S(1)} fusion(bf16[1280,512]{1,0:T(8,128)(2,1)} %all-gather.4.cloned.1.call-done, bf16[2048,512]{1,0:T(8,128)(2,1)} %reshape.119), kind=kOutput, calls=%fused_computation.80 | convolution fusion | flops 2684354560 | bytes 13893632 | tf_op jit(solution)/shard_map/qc,kc->qk/dot_general | solution.py:77
  69.1 4.1 %fusion.50 = (f32[2048]{0:T(1024)S(1)}, f32[2048,1280]{0,1:T(8,128)S(1)}) fusion(f32[1280,2048]{1,0:T(8,128)S(1)} %fusion.51, bf16[1280,64]{0,1:T(8,128)(2,1)S(1)} %reshape.143, bf16[2048,64]{1,0:T(8,128)(2,1)S(1)} %reshape.120, s32[2048]{0:T(1024)S(1)} %fusion.40, s32[1280]{0:T(1024)S(1)} %fusion.38, pred[1280]{0:T(1024)(128)(4,1)S(1)} %fusion.45), kind=kOutput, calls=%fused_computation.79 | convolution fusion | flops 351270912 | bytes 21420288 | tf_op jit(solution)/shard_map/qc,kc->qk/dot_general | solution.py:80
  73.2 3.9 %fusion = f32[2048]{0:T(1024)S(1)} fusion(f32[2048,1280]{0,1:T(8,128)S(1)} %get-tuple-element.3, f32[2048]{0:T(1024)S(1)} %broadcast_maximum_fusion, s32[2048]{0:T(1024)S(1)} %fusion.40, s32[1280]{0:T(1024)S(1)} %fusion.38, pred[1280]{0:T(1024)(128)(4,1)S(1)} %fusion.45), kind=kLoop, calls=%fused_computation.7 | loop fusion | flops 13105152 | bytes 10516736 | tf_op jit(solution)/shard_map/reduce_sum | solution.py:85
  77.2 0.0 copy-start
  77.2 4.5 %divide_convert_fusion = bf16[2048,512]{1,0:T(8,128)(2,1)S(1)} fusion(f32[2048]{0:T(1024)S(1)} %fusion, bf16[1280,512]{1,0:T(8,128)(2,1)S(1)} %copy-done.13, f32[2048,1280]{0,1:T(8,128)S(1)} %get-tuple-element.3, f32[2048]{0:T(1024)S(1)} %broadcast_maximum_fusion, s32[2048]{0:T(1024)S(1)} %fusion.40, s32[1280]{0:T(1024)S(1)} %fusion.38, ...), kind=kOutput, calls=%fused_computation.15 | convolution fusion | flops 2699558912 | bytes 13924608 | tf_op jit(solution)/shard_map/dot_general | solution.py:86
  81.7 0.0 copy-done
  81.8 2.5 fusion.23
  84.3 0.9 copy.73
  85.2 0.0 all-gather.6.cloned.1.call-update
  85.2 0.0 copy-start.9
  85.2 0.0 copy-start.5
  85.2 0.0 reduce-scatter.3.cloned.1.call-start
  85.3 45.7 %all-gather.6.cloned.1.call-done = bf16[256,4096]{1,0:T(8,128)(2,1)} async-done(((bf16[64,4096]{1,0:T(8,128)(2,1)}), bf16[256,4096]{1,0:T(8,128)(2,1)}) %all-gather.6.cloned.1.call-update) | async-done | bytes 2097168 | tf_op jit(solution)/shard_map/all_gather | solution.py:94
  131.0 10.7 %convolution_convert_fusion.2 = bf16[256,1792]{1,0:T(8,128)(2,1)} fusion(bf16[256,4096]{1,0:T(8,128)(2,1)} %all-gather.6.cloned.1.call-done, bf16[4096,1792]{1,0:T(8,128)(2,1)} %param.27), kind=kOutput, calls=%fused_computation.21 | convolution fusion | flops 3758555136 | bytes 17694720 | tf_op jit(solution)/shard_map/dot_general | solution.py:97
  141.7 0.0 reduce-scatter.3.cloned.1.call-update
  141.7 0.3 reduce-scatter.5.cloned.1.call-start
  142.0 0.1 copy.63
  142.1 0.1 eq.31
  142.2 0.1 fusion.35
  142.3 0.2 reduce_window_sum.11
  142.5 0.2 select_reduce_fusion.1
  142.6 0.1 reduce_sum.49
  142.8 0.1 copy.64
  142.9 0.1 fusion.34
  143.0 21.6 %reduce-scatter.3.cloned.1.call-done = bf16[64,1792]{1,0:T(8,128)(2,1)} async-done(((bf16[256,1792]{1,0:T(8,128)(2,1)}), bf16[64,1792]{1,0:T(8,128)(2,1)}) %reduce-scatter.3.cloned.1.call-update) | async-done | bytes 229392 | tf_op jit(solution)/shard_map/reduce_scatter | solution.py:96
  164.6 1.0 add_convert_fusion
  165.6 0.0 copy-start.3
  165.6 21.0 %all_gather.23 = bf16[64,7168]{1,0:T(8,128)(2,1)S(1)} all-gather(bf16[64,1792]{1,0:T(8,128)(2,1)S(1)} %add_convert_fusion), channel_id=1, replica_groups=mesh['groups'=2,'seq'=4,'expert'=4] {'seq'}, dimensions={1}, use_global_device_ids=true | all-gather | bytes 1146880 | tf_op jit(solution)/shard_map/all_gather | solution.py:118
  186.7 0.3 fusion.16
  187.0 0.0 copy-start.1
  187.0 0.8 convolution_convert_fusion.1
  187.8 30.4 %all_to_all.10 = bf16[4,40,7168]{2,1,0:T(8,128)(2,1)S(1)} all-to-all(bf16[4,40,7168]{2,1,0:T(8,128)(2,1)S(1)} %bitcast.51), channel_id=1, replica_groups=mesh['groups'=2,'seq'=4,'expert'=4] {'expert'}, dimensions={0} | all-to-all | bytes 4587520 | tf_op jit(solution)/shard_map/all_to_all | solution.py:126
  218.2 0.8 fusion.12
  219.0 1.3 copy-done.11
  220.2 0.8 fusion.29
  221.0 1.3 copy-done.12
  222.3 2.2 convolution_convert_fusion
  224.5 0.0 reduce-scatter.5.cloned.1.call-update
  224.5 45.8 %reduce-scatter.5.cloned.1.call-done = bf16[4,40,1792]{2,1,0:T(8,128)(2,1)} async-done(((bf16[4,40,7168]{2,1,0:T(8,128)(2,1)}), bf16[4,40,1792]{2,1,0:T(8,128)(2,1)}) %reduce-scatter.5.cloned.1.call-update) | async-done | bytes 573456 | tf_op jit(solution)/shard_map/reduce_scatter | solution.py:20
  270.3 3.5 %all-to-all-start.1 = ((bf16[4,40,1792]{2,1,0:T(8,128)(2,1)}), bf16[4,40,1792]{2,1,0:T(8,128)(2,1)S(1)}, u32[]{:S(2)}, u32[]{:S(2)}) async-start(bf16[4,40,1792]{2,1,0:T(8,128)(2,1)} %reduce-scatter.5.cloned.1.call-done), calls=%async_computation.3 | async-start | bytes 1146880 | tf_op jit(solution)/shard_map/all_to_all | solution.py:23
  273.8 0.1 select_reduce_fusion
  273.9 9.2 %all-to-all-done.1 = bf16[4,40,1792]{2,1,0:T(8,128)(2,1)S(1)} async-done(((bf16[4,40,1792]{2,1,0:T(8,128)(2,1)}), bf16[4,40,1792]{2,1,0:T(8,128)(2,1)S(1)}, u32[]{:S(2)}, u32[]{:S(2)}) %all-to-all-start.1) | async-done | bytes 573472 | tf_op jit(solution)/shard_map/all_to_all | solution.py:23
  283.1 1.1 convolution_convert_fusion.3
  (29 shorter events, 0.2 us)
Async XLA Ops:
  7.2 20.2 %copy-start.2 = (bf16[64,16384]{1,0:T(8,128)(2,1)S(1)}, bf16[64,16384]{1,0:T(8,128)(2,1)}, u32[]{:S(2)}) copy-start(bf16[64,16384]{1,0:T(8,128)(2,1)} %param.17) | copy-start | bytes 6291460
  7.2 57.0 %all-gather.4.cloned.1.call-start = ((), (), s32[]{:S(2)}) async-start(), calls=%async_computation.4 | async-start | bytes 1638400 | tf_op jit(solution)/shard_map/all_gather | solution.py:69
  23.3 6.4 %copy-start.8 = (bf16[32,64]{1,0:T(8,128)(2,1)S(1)}, bf16[32,64]{1,0:T(8,128)(2,1)}, u32[]{:S(2)}) copy-start(bf16[32,64]{1,0:T(8,128)(2,1)} %param.22) | copy-start | bytes 12292
  24.5 19.3 %copy-start.6 = (bf16[256,64]{0,1:T(8,128)(2,1)S(1)}, bf16[256,64]{0,1:T(8,128)(2,1)}, u32[]{:S(2)}) copy-start(bf16[256,64]{0,1:T(8,128)(2,1)} %param.20) | copy-start | bytes 98308
  24.5 19.5 %copy-start.7 = (bf16[64,64]{1,0:T(8,128)(2,1)S(1)}, bf16[64,64]{1,0:T(8,128)(2,1)}, u32[]{:S(2)}) copy-start(bf16[64,64]{1,0:T(8,128)(2,1)} %param.25) | copy-start | bytes 24580
  25.6 34.0 %copy-start.4 = (bf16[64,2048]{1,0:T(8,128)(2,1)S(1)}, bf16[64,2048]{1,0:T(8,128)(2,1)}, u32[]{:S(2)}) copy-start(bf16[64,2048]{1,0:T(8,128)(2,1)} %param.18) | copy-start | bytes 786436
  27.3 103.7 %all-gather.6.cloned.1.call-start = ((), (), s32[]{:S(2)}) async-start(), calls=%async_computation.5 | async-start | bytes 2621440 | tf_op jit(solution)/shard_map/all_gather | solution.py:94
  73.2 4.0 %copy-start.13 = (bf16[1280,512]{1,0:T(8,128)(2,1)S(1)}, bf16[1280,512]{1,0:T(8,128)(2,1)}, u32[]{:S(2)}) copy-start(bf16[1280,512]{1,0:T(8,128)(2,1)} %all-gather.4.cloned.1.call-done) | copy-start | bytes 3932164
  77.2 4.6 %copy-start = (bf16[32,512,128]{2,1,0:T(8,128)(2,1)S(1)}, bf16[32,512,128]{2,1,0:T(8,128)(2,1)}, u32[]{:S(2)}) copy-start(bf16[32,512,128]{2,1,0:T(8,128)(2,1)} %param.26) | copy-start | bytes 12582916
  85.2 56.8 %copy-start.9 = (s32[64,2]{0,1:T(2,128)S(1)}, s32[64,2]{0,1:T(2,128)}, u32[]{:S(2)}) copy-start(s32[64,2]{0,1:T(2,128)} %param.29) | copy-start | bytes 1540
  85.2 79.4 %copy-start.5 = (bf16[64,1792]{1,0:T(8,128)(2,1)S(1)}, bf16[64,1792]{1,0:T(8,128)(2,1)}, u32[]{:S(2)}) copy-start(bf16[64,1792]{1,0:T(8,128)(2,1)} %param.28) | copy-start | bytes 688132
  85.2 79.4 %reduce-scatter.3.cloned.1.call-start = ((), (), s32[]{:S(2)}) async-start(), calls=%async_computation.6 | async-start | bytes 1146880 | tf_op jit(solution)/shard_map/reduce_scatter | solution.py:96
  141.7 128.6 %reduce-scatter.5.cloned.1.call-start = ((), (), s32[]{:S(2)}) async-start(), calls=%async_computation.7 | async-start | bytes 2867200 | tf_op jit(solution)/shard_map/reduce_scatter | solution.py:20
  165.6 52.6 %copy-start.3 = (bf16[64,1792]{1,0:T(8,128)(2,1)}, bf16[64,1792]{1,0:T(8,128)(2,1)S(1)}, u32[]{:S(2)}) copy-start(bf16[64,1792]{1,0:T(8,128)(2,1)S(1)} %add_convert_fusion) | copy-start | bytes 688132
  187.0 31.2 %copy-start.1 = (bf16[1,7168,256]{2,1,0:T(8,128)(2,1)S(1)}, bf16[1,7168,256]{2,1,0:T(8,128)(2,1)}, u32[]{:S(2)}) copy-start(bf16[1,7168,256]{2,1,0:T(8,128)(2,1)} %param.31) | copy-start | bytes 11010052
  218.2 2.0 copy-start.11
  220.2 2.0 copy-start.12
  222.3 51.5 %copy-start.10 = (f32[64,2]{0,1:T(2,128)S(1)}, f32[64,2]{0,1:T(2,128)}, u32[]{:S(2)}) copy-start(f32[64,2]{0,1:T(2,128)} %param.30) | copy-start | bytes 1540
  270.3 12.8 %all-to-all-start.1 = ((bf16[4,40,1792]{2,1,0:T(8,128)(2,1)}), bf16[4,40,1792]{2,1,0:T(8,128)(2,1)S(1)}, u32[]{:S(2)}, u32[]{:S(2)}) async-start(bf16[4,40,1792]{2,1,0:T(8,128)(2,1)} %reduce-scatter.5.cloned.1.call-done), calls=%async_computation.3 | async-start | bytes 1146880 | tf_op jit(solution)/shard_map/all_to_all | solution.py:23
Sparse Core Ops, SparseCore 0:
  27.4 36.6 all-gather.3
  85.3 45.5 all-gather.5
  141.8 22.7 reduce-scatter.2
  224.6 45.5 reduce-scatter.4
where the time goes:
time: 291 us
  waiting for transfers between devices  126 us (43%)
  blocking collectives  95.1 us (33%)
  matrix products  32.4 us (11%)
  between operations  14.9 us (5%)
  local copies, waits for them, and re-layouts  9.37 us (3%)
  other arithmetic  8.86 us (3%)
  starting transfers between devices  3.86 us (1%)
    reduce_scatter x1, waiting for transfers between devices, run_expert(): lax.psum_scatter(partial_out.astype(jnp.bfloat16), 'seq', scatter_dimensi...  45.8 us
    all_gather x1, waiting for transfers between devices, on_device(): all_values = lax.all_gather(head_vals, 'seq', axis=0, tiled=True)  45.7 us
    all_to_all x1, blocking collectives, on_device(): lax.all_to_all(outgoing, 'expert', split_axis=0, concat_axis=0, tiled=True)  30.4 us
    reduce_scatter x1, waiting for transfers between devices, on_device(): lax.psum_scatter(jnp.dot(all_values, w_out, preferred_element_type=jnp.fl...  21.6 us
    all_gather x1, blocking collectives, on_device(): lax.all_gather(attn_residual, 'seq', axis=1, tiled=True).astype(jnp.float32)  21 us
    all_gather x1, blocking collectives, on_device(): lax.all_gather(tool_lat, 'seq', axis=0, tiled=True)  15.3 us
    all_gather x1, blocking collectives, on_device(): piece_rope = lax.all_gather(local_rope, 'seq', axis=0, tiled=True)  15.2 us
    all_gather x1, blocking collectives, on_device(): lax.all_gather(tool_rope, 'seq', axis=0, tiled=True)  13.2 us
  transfers between devices with their start and end apart: 5, of which 5 were waited for; matrix products, arithmetic and copies ran while one was open for 2% of the time, Pallas kernels for 0%

commit v1 on v0

v1 whole, which is shorter than its diff:
```python
import functools

import jax
import jax.numpy as jnp
from jax import lax
from jax.experimental import pallas as pl
from jax.experimental.pallas import tpu as pltpu
from jax.sharding import PartitionSpec as P

MESH = pl.DeviceIdType.MESH
norm_eps = 1e-06
exp2_scale = 192.0 ** (-0.5) * 1.4426950408889634
floor_score = -1e30
lanes = 128


def dot(a, b):
    return jnp.dot(a, b, preferred_element_type=jnp.float32)


def dot_nt(a, b):
    return lax.dot_general(a, b, (((1,), (1,)), ((), ())), preferred_element_type=jnp.float32)


def column_tile(width):
    return 256 if width % 256 == 0 else 128


def layer_kernel(
    dims,
    offset_ref, kv_ref, qr_ref, resid_ref, routes_ref, probs_ref,
    q_hbm, wuv_hbm, wout_hbm, wg_hbm, wu_hbm, wd_hbm,
    attn_ref, mix_ref,
    q_buf, wuv, wout, wg, wu, wd,
    kx, tool_buf, keys, wts, allv, oacc,
    p1, rc1, q1, ry1, xg, p2, rc2, q2, ry2, t2, rz2,
    q_sem, w_sem,
    kz_s, ky_s, kc_s, k_r,
    wt_s, wt_r,
    v_s, v_r,
    o_s, oc_r, oy_r,
    xz_s, xy_s, xc_s, x_r,
    pc_s, pc_r, py_s, py_r, pz_s, pz_r,
):
    S, E, G, ctx_dev, tool_dev = dims
    Y = E // 2
    heads, T, LAT = q_buf.shape
    VD = wuv.shape[2]
    n = heads // G
    GV = G * VD
    TOK, C = resid_ref.shape
    ctx, tool_len = S * ctx_dev, S * tool_dev
    suf = S * T
    rope = qr_ref.shape[1] // heads
    s = lax.axis_index("seq")
    e = lax.axis_index("expert")
    y, c = lax.div(e, 2), lax.rem(e, 2)
    sister = e + 1 - 2 * c

    def seq_at(d):
        return lax.rem(s + d, S)

    def y_at(d):
        return lax.rem(y + d, Y)

    pending = []

    def send(src, dst, send_sem, recv_sem, **where):
        copy = pltpu.make_async_remote_copy(
            src_ref=src, dst_ref=dst, send_sem=send_sem, recv_sem=recv_sem,
            device_id=where, device_id_type=MESH,
        )
        copy.start()
        return copy

    def arrived(dst, sem):
        pltpu.make_async_remote_copy(
            src_ref=dst, dst_ref=dst, send_sem=sem, recv_sem=sem,
            device_id={"expert": sister}, device_id_type=MESH,
        ).wait_recv()

    barrier = pltpu.get_barrier_semaphore()
    for d in range(1, S):
        pl.semaphore_signal(barrier, inc=1, device_id={"seq": seq_at(d)}, device_id_type=MESH)
    for d in range(1, E):
        pl.semaphore_signal(
            barrier, inc=1, device_id={"expert": lax.rem(e + d, E)}, device_id_type=MESH
        )

    def q_copy(h):
        return pltpu.make_async_copy(
            q_hbm.at[:, pl.ds(pl.multiple_of(h * LAT, LAT), LAT)], q_buf.at[h], q_sem.at[h]
        )

    def start_q(h, carry):
        q_copy(h).start()
        return carry

    loads = [
        pltpu.make_async_copy(a, b, w_sem.at[i])
        for i, (a, b) in enumerate(
            ((wuv_hbm, wuv), (wout_hbm, wout), (wg_hbm.at[0], wg), (wu_hbm.at[0], wu), (wd_hbm.at[0], wd))
        )
    ]
    kx[s, e] = kv_ref[...]
    lane_tok = lax.broadcasted_iota(jnp.int32, (TOK, lanes), 1)
    routes = routes_ref[...]
    probs = probs_ref[...]
    weight = 2.5 * probs / jnp.sum(probs, axis=1, keepdims=True)
    mine = jnp.zeros((TOK, lanes), jnp.float32)
    for k in range(routes.shape[1]):
        mine = mine + jnp.where(routes[:, k : k + 1] == lane_tok, weight[:, k : k + 1], 0.0)
    wts[e] = mine

    pl.semaphore_wait(barrier, S - 1 + E - 1)

    def gather_start(buf, zs, rs):
        for d in range(1, S):
            pending.append(send(buf.at[s, e], buf.at[s, e], zs.at[d], rs.at[s, e], seq=seq_at(d)))

    def gather_forward(buf, ys, cs, rs):
        for i in range(S):
            so = seq_at(i)
            if i > 0:
                arrived(buf.at[so, e], rs.at[so, e])
            for d in range(1, Y):
                pending.append(
                    send(buf.at[so, e], buf.at[so, e], ys.at[i, d], rs.at[so, e], expert=y_at(d) * 2 + c)
                )
            pending.append(send(buf.at[so, e], buf.at[so, e], cs.at[i, 0], rs.at[so, e], expert=sister))
        for i in range(S):
            so = seq_at(i)
            for d in range(1, Y):
                eo = y_at(d) * 2 + c
                arrived(buf.at[so, eo], rs.at[so, eo])
                pending.append(
                    send(buf.at[so, eo], buf.at[so, eo], cs.at[i, d], rs.at[so, eo], expert=sister)
                )

    def gather_end(buf, rs, i):
        so = seq_at(i)
        for d in range(Y):
            eo = y_at(d) * 2 + 1 - c
            arrived(buf.at[so, eo], rs.at[so, eo])

    gather_start(kx, kz_s, k_r)
    for d in range(1, E):
        pending.append(
            send(wts.at[e], wts.at[e], wt_s.at[d], wt_r.at[e], expert=lax.rem(e + d, E))
        )
    lax.fori_loop(0, heads, start_q, 0)
    for load in loads:
        load.start()
    gather_forward(kx, ky_s, kc_s, k_r)
    for i in range(S):
        gather_end(kx, k_r, i)

    width = kx.shape[3]
    for so in range(S):
        block = kx[so].reshape(E * kx.shape[2], width)
        tool_buf[so * tool_dev : (so + 1) * tool_dev] = block[ctx_dev + T : ctx_dev + T + tool_dev]
        keys[ctx + so * T : ctx + (so + 1) * T] = block[ctx_dev : ctx_dev + T]
        keys[so * ctx_dev : (so + 1) * ctx_dev] = block[:ctx_dev]
    offset = offset_ref[0]
    tool_all = tool_buf[...]
    for so in range(S):
        rows = slice(so * ctx_dev, (so + 1) * ctx_dev)
        shifted = so * ctx_dev + lax.broadcasted_iota(jnp.int32, (ctx_dev, tool_len), 0) - offset
        column = lax.broadcasted_iota(jnp.int32, (ctx_dev, tool_len), 1)
        pick = jnp.where(shifted == column, 1.0, 0.0).astype(jnp.bfloat16)
        inside = jnp.sum(pick.astype(jnp.float32), axis=1, keepdims=True) > 0.5
        keys[rows] = jnp.where(
            inside, dot(pick, tool_all), keys[rows].astype(jnp.float32)
        ).astype(jnp.bfloat16)

    def wait_q(h, carry):
        q_copy(h).wait()
        return carry

    lax.fori_loop(0, heads, wait_q, 0)
    loads[0].wait()

    lane_q = lax.broadcasted_iota(jnp.int32, (T, lanes), 1)
    rows_g = G * T
    query_pos = s * T + lax.rem(lax.broadcasted_iota(jnp.int32, (rows_g, suf), 0), T)
    hidden = lax.broadcasted_iota(jnp.int32, (rows_g, suf), 1) > query_pos

    def v_copy(k, d):
        return pltpu.make_async_remote_copy(
            src_ref=allv.at[k, s], dst_ref=allv.at[k, s], send_sem=v_s.at[k, d],
            recv_sem=v_r.at[k, s], device_id={"seq": seq_at(d)}, device_id_type=MESH,
        )

    def attend(k, carry):
        q = q_buf[pl.ds(k * G, G)].reshape(rows_g, LAT)
        step = G * rope
        turned = qr_ref[:, pl.ds(pl.multiple_of(k * step, step), step)].astype(jnp.float32)
        parts = []
        for j in range(G):
            low = j * rope % lanes
            at = j * rope // lanes * lanes
            keep = (lane_q >= low) & (lane_q < low + rope)
            parts.append(jnp.where(keep, turned[:, at : at + lanes], 0.0))
        qr = jnp.concatenate(parts, axis=0).astype(jnp.bfloat16)
        s1 = dot_nt(q, keys[:ctx, :LAT]) + dot_nt(qr, keys[:ctx, LAT:])
        s2 = dot_nt(q, keys[ctx:, :LAT]) + dot_nt(qr, keys[ctx:, LAT:])
        s2 = jnp.where(hidden, floor_score, s2)
        top = jnp.maximum(
            jnp.max(s1, axis=1, keepdims=True), jnp.max(s2, axis=1, keepdims=True)
        )
        e1 = jnp.exp2((s1 - top) * exp2_scale)
        e2 = jnp.exp2((s2 - top) * exp2_scale)
        total = jnp.sum(e1, axis=1, keepdims=True) + jnp.sum(e2, axis=1, keepdims=True)
        acc = dot(e1.astype(jnp.bfloat16), keys[:ctx, :LAT])
        acc = acc + dot(e2.astype(jnp.bfloat16), keys[ctx:, :LAT])
        out = (acc / total).astype(jnp.bfloat16)
        for j in range(G):
            allv[k, s, :, j * VD : (j + 1) * VD] = dot(
                out[j * T : (j + 1) * T], wuv[k * G + j]
            ).astype(jnp.bfloat16)
        for d in range(1, S):
            v_copy(k, d).start()
        return carry

    lax.fori_loop(0, n, attend, 0)

    loads[1].wait()
    oacc[...] = jnp.zeros_like(oacc)
    tile = column_tile(C)

    def project(k, carry):
        for d in range(1, S):
            so = seq_at(d)
            arrived(allv.at[k, so], v_r.at[k, so])
        values = allv[k].reshape(suf, GV)
        at = pl.ds(pl.multiple_of(k * GV, GV), GV)
        for j in range(0, C, tile):
            oacc[:, j : j + tile] += dot(values, wout[at, j : j + tile])
        return carry

    lax.fori_loop(0, n, project, 0)

    for yy in range(Y):
        for cc in range(2):
            b = yy * 2 + cc
            p1[cc, yy] = oacc[b * TOK : (b + 1) * TOK].astype(jnp.bfloat16)
    pending.append(send(p1.at[1 - c], rc1, o_s.at[0], oc_r, expert=sister))
    arrived(rc1, oc_r)
    for yy in range(Y):
        q1[yy] = (p1[c, yy].astype(jnp.float32) + rc1[yy].astype(jnp.float32)).astype(jnp.bfloat16)
    for d in range(1, Y):
        yo = y_at(d)
        pending.append(send(q1.at[yo], ry1.at[y], o_s.at[d], oy_r.at[y], expert=yo * 2 + c))
    summed = resid_ref[...].astype(jnp.float32) + q1[y].astype(jnp.float32)
    for d in range(1, Y):
        yo = y_at(d)
        arrived(ry1.at[yo], oy_r.at[yo])
        summed = summed + ry1[yo].astype(jnp.float32)
    stream = summed.astype(jnp.bfloat16)
    xg[s, e] = stream
    gather_start(xg, xz_s, x_r)
    attn_ref[...] = stream

    for d in range(1, E):
        eo = lax.rem(e + d, E)
        arrived(wts.at[eo], wt_r.at[eo])
    rows_all = E * TOK
    lane_all = lax.broadcasted_iota(jnp.int32, (rows_all, lanes), 1)
    own_weight = jnp.sum(
        jnp.where(lane_all == e, wts[...].reshape(rows_all, lanes), 0.0), axis=1, keepdims=True
    )
    gather_forward(xg, xy_s, xc_s, x_r)

    loads[2].wait()
    loads[3].wait()
    square = jnp.zeros((rows_all, 1), jnp.float32)
    gate = jnp.zeros((rows_all, wg.shape[1]), jnp.float32)
    upper = jnp.zeros((rows_all, wg.shape[1]), jnp.float32)
    for i in range(S):
        gather_end(xg, x_r, i)
        so = seq_at(i)
        x = xg[so].reshape(rows_all, C)
        at = pl.ds(pl.multiple_of(so * C, C), C)
        wide = x.astype(jnp.float32)
        square = square + jnp.sum(wide * wide, axis=1, keepdims=True)
        gate = gate + dot(x, wg[at, :])
        upper = upper + dot(x, wu[at, :])
    inv = lax.rsqrt(square * (1.0 / (S * C)) + norm_eps)
    gate = gate * inv
    inner = (gate / (1.0 + jnp.exp(-gate)) * (upper * inv) * own_weight).astype(jnp.bfloat16)

    loads[4].wait()
    for i in range(S):
        so = seq_at(i + 1)
        for j in range(0, C, tile):
            part = dot(inner, wd[:, pl.ds(pl.multiple_of(so * C + j, 128), tile)]).astype(jnp.bfloat16)
            for yy in range(Y):
                for cc in range(2):
                    b = yy * 2 + cc
                    p2[so, cc, yy, :, j : j + tile] = part[b * TOK : (b + 1) * TOK]
        pending.append(send(p2.at[so, 1 - c], rc2.at[so], pc_s.at[i], pc_r.at[so], expert=sister))
    for i in range(S):
        so = seq_at(i + 1)
        arrived(rc2.at[so], pc_r.at[so])
        for d in range(1, Y + 1):
            yo = y_at(d)
            q2[so, yo] = (
                p2[so, c, yo].astype(jnp.float32) + rc2[so, yo].astype(jnp.float32)
            ).astype(jnp.bfloat16)
            if d < Y:
                pending.append(
                    send(q2.at[so, yo], ry2.at[so, y], py_s.at[i, d], py_r.at[so, y], expert=yo * 2 + c)
                )
    mixed = None
    for i in range(S):
        so = seq_at(i + 1)
        mixed = q2[so, y].astype(jnp.float32)
        for d in range(1, Y):
            yo = y_at(d)
            arrived(ry2.at[so, yo], py_r.at[so, yo])
            mixed = mixed + ry2[so, yo].astype(jnp.float32)
        if i < S - 1:
            t2[so] = mixed.astype(jnp.bfloat16)
            pending.append(send(t2.at[so], rz2.at[s], pz_s.at[i], pz_r.at[s], seq=so))
    for d in range(1, S):
        so = seq_at(S - d)
        arrived(rz2.at[so], pz_r.at[so])
        mixed = mixed + rz2[so].astype(jnp.float32)
    mix_ref[...] = mixed.astype(jnp.bfloat16)

    for copy in pending:
        copy.wait_send()

    def drain(k, carry):
        for d in range(1, S):
            v_copy(k, d).wait_send()
        return carry

    lax.fori_loop(0, n, drain, 0)


def on_device(
    q_lat, q_rope, cache_lat, cache_rope, tool_lat, tool_rope, offset, suf_lat, suf_rope,
    w_uv, w_out, resid, routes, probs, w_gate, w_up, w_down,
):
    S, E = lax.axis_size("seq"), lax.axis_size("expert")
    Y = E // 2
    T = q_lat.shape[0]
    heads, LAT, VD = w_uv.shape
    rope = cache_rope.shape[1]
    ctx_dev, tool_dev = cache_lat.shape[0], tool_lat.shape[0]
    TOK, C = resid.shape
    G = max(g for g in range(1, heads + 1) if heads % g == 0 and g * T <= max(256, 2 * T) and g * rope % lanes == 0)
    n = heads // G
    F = w_gate.shape[2]
    latents = jnp.concatenate([cache_lat, suf_lat, tool_lat], axis=0)
    turned = jnp.concatenate([cache_rope, suf_rope, tool_rope], axis=0)
    packed = jnp.concatenate([latents] + [turned] * (lanes // rope), axis=1)
    total = packed.shape[0]
    piece = -(-total // (16 * E)) * 16
    packed = jnp.pad(packed, ((0, piece * E - total), (0, 0)))
    own = lax.dynamic_slice_in_dim(packed, lax.axis_index("expert") * piece, piece, axis=0)
    width = packed.shape[1]
    bf, f32 = jnp.bfloat16, jnp.float32
    dma, vmem = pltpu.SemaphoreType.DMA, pltpu.VMEM
    in_vmem = pl.BlockSpec(memory_space=pltpu.VMEM)
    anywhere = pl.BlockSpec(memory_space=pl.ANY)
    scratch = [
        vmem((heads, T, LAT), bf), vmem(w_uv.shape, bf), vmem(w_out.shape, bf),
        vmem(w_gate.shape[1:], bf), vmem(w_up.shape[1:], bf), vmem(w_down.shape[1:], bf),
        vmem((S, E, piece, width), bf), vmem((S * tool_dev, width), bf),
        vmem((S * (ctx_dev + T), width), bf), vmem((E, TOK, lanes), f32),
        vmem((n, S, T, G * VD), bf), vmem((S * T, C), f32),
        vmem((2, Y, TOK, C), bf), vmem((Y, TOK, C), bf), vmem((Y, TOK, C), bf), vmem((Y, TOK, C), bf),
        vmem((S, E, TOK, C), bf),
        vmem((S, 2, Y, TOK, C), bf), vmem((S, Y, TOK, C), bf), vmem((S, Y, TOK, C), bf),
        vmem((S, Y, TOK, C), bf), vmem((S, TOK, C), bf), vmem((S, TOK, C), bf),
        dma((heads,)), dma((5,)),
        dma((S,)), dma((S, Y)), dma((S, Y)), dma((S, E)),
        dma((E,)), dma((E,)),
        dma((n, S)), dma((n, S)),
        dma((Y,)), dma, dma((Y,)),
        dma((S,)), dma((S, Y)), dma((S, Y)), dma((S, E)),
        dma((S,)), dma((S,)), dma((S, Y)), dma((S, Y)), dma((S,)), dma((S,)),
    ]
    return pl.pallas_call(
        functools.partial(layer_kernel, (S, E, G, ctx_dev, tool_dev)),
        out_shape=(jax.ShapeDtypeStruct((TOK, C), bf), jax.ShapeDtypeStruct((TOK, C), bf)),
        in_specs=[pl.BlockSpec(memory_space=pltpu.SMEM)] + [in_vmem] * 5 + [anywhere] * 6,
        out_specs=(in_vmem, in_vmem),
        scratch_shapes=scratch,
        compiler_params=pltpu.CompilerParams(
            collective_id=0, has_side_effects=True, vmem_limit_bytes=61 * 1024 * 1024
        ),
    )(offset, own, q_rope, resid, routes, probs, q_lat, w_uv, w_out, w_gate, w_up, w_down)


def solution(mesh):
    placed = (
        P(("groups", "seq"), "expert"),
        P(("groups", "seq"), "expert"),
        P(("groups", "seq"), None),
        P(("groups", "seq"), None),
        P(("groups", "seq"), None),
        P(("groups", "seq"), None),
        P("groups"),
        P(("groups", "seq"), None),
        P(("groups", "seq"), None),
        P("expert", None, None),
        P("expert", "seq"),
        P(("groups", "expert"), "seq"),
        P(("groups", "expert"), None),
        P(("groups", "expert"), None),
        P("expert", None, "seq"),
        P("expert", None, "seq"),
        P("expert", "seq", None),
    )
    return jax.shard_map(
        on_device,
        mesh=mesh,
        in_specs=placed,
        out_specs=(P(("groups", "expert"), "seq"), P(("groups", "expert"), "seq")),
        check_vma=False,
    )
```

time: 291 us -> 164 us (0.56)
  Pallas kernels: 0 us -> 153 us
  waiting for transfers between devices: 126 us -> 0 us
  blocking collectives: 95.1 us -> 0 us
  matrix products: 32.4 us -> 0 us
  between operations: 14.9 us -> 1.29 us
  other arithmetic: 8.86 us -> 2.07 us
  starting transfers between devices: 3.86 us -> 0 us
    pallas_call x0 -> x1, Pallas kernels: none -> 153 us  [on_device(): pl.pallas_call(functools.partial(layer_kernel, (S, E, G, ctx_dev, tool_de...]
    reduce_scatter x2 -> x0, waiting for transfers between devices: 67.4 us -> none  [the longest x1 45.8 us: run_expert(): lax.psum_scatter(partial_out.astype(jnp.bfloat16), 'seq', scatter_dimensi...]
    all_gather x4 -> x0, blocking collectives: 64.7 us -> none  [the longest x1 21 us: on_device(): lax.all_gather(attn_residual, 'seq', axis=1, tiled=True).astype(jnp.float32)]
    all_gather x2 -> x0, waiting for transfers between devices: 49.6 us -> none  [the longest x1 45.7 us: on_device(): all_values = lax.all_gather(head_vals, 'seq', axis=0, tiled=True)]
    dot_general x10 -> x0, matrix products: 32.4 us -> none  [the longest x1 10.7 us: on_device(): jnp.dot(all_values, w_out, preferred_element_type=jnp.float32)]
    all_to_all x1 -> x0, blocking collectives: 30.4 us -> none  [on_device(): lax.all_to_all(outgoing, 'expert', split_axis=0, concat_axis=0, tiled=True)]
    all_to_all x1 -> x0, waiting for transfers between devices: 9.18 us -> none  [run_expert(): lax.all_to_all(summed, 'expert', split_axis=0, concat_axis=0, tiled=True)]
    reduce_sum x5 -> x0, other arithmetic: 4.52 us -> none  [the longest x1 3.94 us: on_device(): new_total = jnp.sum(weights, axis=1)]
  transfers between devices with their start and end apart: 5 -> 0, of which waited for: 5 -> 0; matrix products, arithmetic and copies ran while one was open for 2% -> 0% of each run, Pallas kernels for 0% -> 0%
where the time goes in v1:
time: 164 us
  Pallas kernels  153 us (93%)
  local copies, waits for them, and re-layouts  6.9 us (4%)
  other arithmetic  2.07 us (1%)
    pallas_call x1, Pallas kernels, on_device(): pl.pallas_call(functools.partial(layer_kernel, (S, E, G, ctx_dev, tool_de...  153 us
    unnamed x5, local copies, waits for them, and re-layouts  6.9 us

profile of v1, /device:TPU:0, one launch (start us, length us, event | category | flops | bytes accessed | tf_op | source)
XLA Modules:
  0.0 163.7 jit_solution(16261656929231850005)
XLA Ops:
  1.3 1.4 copy.20.routes_ref
  2.7 1.4 copy.21.probs_ref
  4.0 0.9 copy.19
  4.9 2.1 %fusion.12.kv_ref = bf16[96,640]{1,0:T(8,128)(2,1)} fusion(s32[]{:T(128)S(6)} %select_n.3, bf16[256,512]{1,0:T(8,128)(2,1)} %param.19, bf16[64,512]{1,0:T(8,128)(2,1)} %param.24, bf16[256,64]{1,0:T(8,128)(2,1)S(1)} %copy.19, bf16[64,64]{1,0:T(8,128)(2,1)} %param.25, bf16[32,512]{1,0:T(8,128)(2,1)} %param.21, bf16[32,64]{1,0:T(8,128)(2,1)} %param.22), kind=kLoop, calls=%fused_computation.22 | loop fusion | flops 1781760 | bytes 529408 | tf_op jit(solution)/shard_map/concatenate | solution.py:358
  7.0 153.4 %shard_map.176 = (bf16[64,1792]{1,0:T(8,128)(2,1)}, bf16[64,1792]{1,0:T(8,128)(2,1)}) custom-call(s32[1]{0:T(128)S(6)} %copy.24.offset_ref, bf16[96,640]{1,0:T(8,128)(2,1)} %fusion.12.kv_ref, bf16[64,2048]{1,0:T(8,128)(2,1)} %qr_ref.1, bf16[64,1792]{1,0:T(8,128)(2,1)} %resid_ref.1, s32[64,2]{1,0:T(8,128)} %copy.20.routes_ref, f32[64,2]{1,0:T(8,128)} %copy.21.probs_ref, ...), custom_call_target="tpu_custom_call" | custom-call | tf_op jit(solution)/shard_map/pallas_call | solution.py:386
  160.4 1.6 %copy.25 = bf16[64,1792]{1,0:T(8,128)(2,1)} copy(bf16[64,1792]{1,0:T(8,128)(2,1)} %get-tuple-element.4) | data formatting | bytes 458752
  162.1 1.6 %copy.26 = bf16[64,1792]{1,0:T(8,128)(2,1)} copy(bf16[64,1792]{1,0:T(8,128)(2,1)} %get-tuple-element.5) | data formatting | bytes 458752

commit v2 on v1

--- a/solution.py
+++ b/solution.py
@@ -71,13 +71,19 @@
             device_id=where, device_id_type=MESH,
         )
         copy.start()
-        return copy
+        return copy.wait_send
 
     def arrived(dst, sem):
         pltpu.make_async_remote_copy(
             src_ref=dst, dst_ref=dst, send_sem=sem, recv_sem=sem,
             device_id={"expert": sister}, device_id_type=MESH,
         ).wait_recv()
+
+    def left(src, sem):
+        pltpu.make_async_remote_copy(
+            src_ref=src, dst_ref=src, send_sem=sem, recv_sem=sem,
+            device_id={"expert": sister}, device_id_type=MESH,
+        ).wait_send()
 
     barrier = pltpu.get_barrier_semaphore()
     for d in range(1, S):
@@ -102,7 +108,7 @@
             ((wuv_hbm, wuv), (wout_hbm, wout), (wg_hbm.at[0], wg), (wu_hbm.at[0], wu), (wd_hbm.at[0], wd))
         )
     ]
-    kx[s, e] = kv_ref[...]
+    kx[s] = kv_ref[...]
     lane_tok = lax.broadcasted_iota(jnp.int32, (TOK, lanes), 1)
     routes = routes_ref[...]
     probs = probs_ref[...]
@@ -114,28 +120,89 @@
 
     pl.semaphore_wait(barrier, S - 1 + E - 1)
 
+    def line(d):
+        return (
+            (s >= d, s - d, s + 1 < S, s + 1, 0),
+            (s + d < S, s + d, s >= 1, s - 1, 1),
+        )
+
+    def send_when(cond, *args, **where):
+        @pl.when(cond)
+        def _():
+            send(*args, **where)
+
+        def finish():
+            @pl.when(cond)
+            def _():
+                pltpu.make_async_remote_copy(
+                    src_ref=args[0], dst_ref=args[1], send_sem=args[2], recv_sem=args[3],
+                    device_id=where, device_id_type=MESH,
+                ).wait_send()
+
+        return finish
+
     def gather_start(buf, zs, rs):
-        for d in range(1, S):
-            pending.append(send(buf.at[s, e], buf.at[s, e], zs.at[d], rs.at[s, e], seq=seq_at(d)))
-
-    def gather_forward(buf, ys, cs, rs):
-        for i in range(S):
-            so = seq_at(i)
-            if i > 0:
-                arrived(buf.at[so, e], rs.at[so, e])
+        own = buf.at[s, e]
+        pending.append(send_when(s + 1 < S, own, own, zs.at[s, 0], rs.at[s, e], seq=s + 1))
+        pending.append(send_when(s >= 1, own, own, zs.at[s, 1], rs.at[s, e], seq=s - 1))
+
+    def gather_forward(buf, zs, ys, cs, rs, with_own):
+        def beside(so):
+            block = buf.at[so, e]
             for d in range(1, Y):
-                pending.append(
-                    send(buf.at[so, e], buf.at[so, e], ys.at[i, d], rs.at[so, e], expert=y_at(d) * 2 + c)
-                )
-            pending.append(send(buf.at[so, e], buf.at[so, e], cs.at[i, 0], rs.at[so, e], expert=sister))
-        for i in range(S):
-            so = seq_at(i)
+                send(block, block, ys.at[so, d], rs.at[so, e], expert=y_at(d) * 2 + c)
+            send(block, block, cs.at[so, 0], rs.at[so, e], expert=sister)
+
+        def onward(so):
             for d in range(1, Y):
                 eo = y_at(d) * 2 + c
-                arrived(buf.at[so, eo], rs.at[so, eo])
-                pending.append(
-                    send(buf.at[so, eo], buf.at[so, eo], cs.at[i, d], rs.at[so, eo], expert=sister)
-                )
+                block = buf.at[so, eo]
+                arrived(block, rs.at[so, eo])
+                send(block, block, cs.at[so, d], rs.at[so, eo], expert=sister)
+
+        if with_own:
+            beside(s)
+        for d in range(1, S):
+            for here, so, more, target, way in line(d):
+                @pl.when(here)
+                def _(so=so, more=more, target=target, way=way):
+                    block = buf.at[so, e]
+                    arrived(block, rs.at[so, e])
+
+                    @pl.when(more)
+                    def _():
+                        send(block, block, zs.at[so, way], rs.at[so, e], seq=target)
+
+                    beside(so)
+        if with_own:
+            onward(s)
+        for d in range(1, S):
+            for here, so, more, target, way in line(d):
+                @pl.when(here)
+                def _(so=so):
+                    onward(so)
+
+        def finish():
+            def sent(so):
+                block = buf.at[so, e]
+                for d in range(1, Y):
+                    left(block, ys.at[so, d])
+                    left(block, cs.at[so, d])
+                left(block, cs.at[so, 0])
+
+            if with_own:
+                sent(s)
+            for d in range(1, S):
+                for here, so, more, target, way in line(d):
+                    @pl.when(here)
+                    def _(so=so, more=more, way=way):
+                        @pl.when(more)
+                        def _():
+                            left(buf.at[so, e], zs.at[so, way])
+
+                        sent(so)
+
+        pending.append(finish)
 
     def gather_end(buf, rs, i):
         so = seq_at(i)
@@ -151,8 +218,8 @@
     lax.fori_loop(0, heads, start_q, 0)
     for load in loads:
         load.start()
-    gather_forward(kx, ky_s, kc_s, k_r)
-    for i in range(S):
+    gather_forward(kx, kz_s, ky_s, kc_s, k_r, False)
+    for i in range(1, S):
         gather_end(kx, k_r, i)
 
     width = kx.shape[3]
@@ -185,13 +252,13 @@
     query_pos = s * T + lax.rem(lax.broadcasted_iota(jnp.int32, (rows_g, suf), 0), T)
     hidden = lax.broadcasted_iota(jnp.int32, (rows_g, suf), 1) > query_pos
 
-    def v_copy(k, d):
+    def v_copy(k, origin, way, target):
         return pltpu.make_async_remote_copy(
-            src_ref=allv.at[k, s], dst_ref=allv.at[k, s], send_sem=v_s.at[k, d],
-            recv_sem=v_r.at[k, s], device_id={"seq": seq_at(d)}, device_id_type=MESH,
-        )
-
-    def attend(k, carry):
+            src_ref=allv.at[k, origin], dst_ref=allv.at[k, origin], send_sem=v_s.at[k, origin, way],
+            recv_sem=v_r.at[k, origin], device_id={"seq": target}, device_id_type=MESH,
+        )
+
+    def attend(k):
         q = q_buf[pl.ds(k * G, G)].reshape(rows_g, LAT)
         step = G * rope
         turned = qr_ref[:, pl.ds(pl.multiple_of(k * step, step), step)].astype(jnp.float32)
@@ -218,27 +285,51 @@
             allv[k, s, :, j * VD : (j + 1) * VD] = dot(
                 out[j * T : (j + 1) * T], wuv[k * G + j]
             ).astype(jnp.bfloat16)
-        for d in range(1, S):
-            v_copy(k, d).start()
-        return carry
-
-    lax.fori_loop(0, n, attend, 0)
-
-    loads[1].wait()
-    oacc[...] = jnp.zeros_like(oacc)
+        for more, target, way in ((s + 1 < S, s + 1, 0), (s >= 1, s - 1, 1)):
+            @pl.when(more)
+            def _(target=target, way=way):
+                v_copy(k, s, way, target).start()
+
     tile = column_tile(C)
 
-    def project(k, carry):
-        for d in range(1, S):
-            so = seq_at(d)
-            arrived(allv.at[k, so], v_r.at[k, so])
+    def project(k):
         values = allv[k].reshape(suf, GV)
         at = pl.ds(pl.multiple_of(k * GV, GV), GV)
         for j in range(0, C, tile):
             oacc[:, j : j + tile] += dot(values, wout[at, j : j + tile])
+
+    oacc[...] = jnp.zeros_like(oacc)
+    loads[1].wait()
+    lag = 2
+
+    def turn(k, carry):
+        @pl.when(k < n)
+        def _():
+            attend(k)
+
+        for d in range(1, S):
+            at = k - lag * d
+
+            @pl.when((at >= 0) & (at < n))
+            def _(at=at, d=d):
+                for here, so, more, target, way in line(d):
+                    @pl.when(here)
+                    def _(so=so, more=more, target=target, way=way):
+                        arrived(allv.at[at, so], v_r.at[at, so])
+
+                        @pl.when(more)
+                        def _():
+                            v_copy(at, so, way, target).start()
+
+        done = k - lag * (S - 1)
+
+        @pl.when(done >= 0)
+        def _():
+            project(done)
+
         return carry
 
-    lax.fori_loop(0, n, project, 0)
+    lax.fori_loop(0, n + lag * (S - 1), turn, 0)
 
     for yy in range(Y):
         for cc in range(2):
@@ -269,7 +360,7 @@
     own_weight = jnp.sum(
         jnp.where(lane_all == e, wts[...].reshape(rows_all, lanes), 0.0), axis=1, keepdims=True
     )
-    gather_forward(xg, xy_s, xc_s, x_r)
+    gather_forward(xg, xz_s, xy_s, xc_s, x_r, True)
 
     loads[2].wait()
     loads[3].wait()
@@ -299,41 +390,71 @@
                     b = yy * 2 + cc
                     p2[so, cc, yy, :, j : j + tile] = part[b * TOK : (b + 1) * TOK]
         pending.append(send(p2.at[so, 1 - c], rc2.at[so], pc_s.at[i], pc_r.at[so], expert=sister))
-    for i in range(S):
+    cut = C // 256 * 128
+    halves = ((0, cut), (cut, C - cut))
+    units = [(i, h) for i in range(S) for h in range(2)]
+    last = [None, None]
+
+    def cores_sum(i, h):
         so = seq_at(i + 1)
-        arrived(rc2.at[so], pc_r.at[so])
+        cols = pl.ds(*halves[h])
+        if h == 0:
+            arrived(rc2.at[so], pc_r.at[so])
         for d in range(1, Y + 1):
             yo = y_at(d)
-            q2[so, yo] = (
-                p2[so, c, yo].astype(jnp.float32) + rc2[so, yo].astype(jnp.float32)
+            q2[so, yo, :, cols] = (
+                p2[so, c, yo, :, cols].astype(jnp.float32) + rc2[so, yo, :, cols].astype(jnp.float32)
             ).astype(jnp.bfloat16)
             if d < Y:
                 pending.append(
-                    send(q2.at[so, yo], ry2.at[so, y], py_s.at[i, d], py_r.at[so, y], expert=yo * 2 + c)
+                    send(
+                        q2.at[so, yo, :, cols], ry2.at[so, y, :, cols],
+                        py_s.at[i, d, h], py_r.at[so, y, h], expert=yo * 2 + c,
+                    )
                 )
-    mixed = None
-    for i in range(S):
+
+    def chips_sum(i, h):
         so = seq_at(i + 1)
-        mixed = q2[so, y].astype(jnp.float32)
+        cols = pl.ds(*halves[h])
+        total = q2[so, y, :, cols].astype(jnp.float32)
         for d in range(1, Y):
             yo = y_at(d)
-            arrived(ry2.at[so, yo], py_r.at[so, yo])
-            mixed = mixed + ry2[so, yo].astype(jnp.float32)
+            arrived(ry2.at[so, yo, :, cols], py_r.at[so, yo, h])
+            total = total + ry2[so, yo, :, cols].astype(jnp.float32)
         if i < S - 1:
-            t2[so] = mixed.astype(jnp.bfloat16)
-            pending.append(send(t2.at[so], rz2.at[s], pz_s.at[i], pz_r.at[s], seq=so))
-    for d in range(1, S):
-        so = seq_at(S - d)
-        arrived(rz2.at[so], pz_r.at[so])
-        mixed = mixed + rz2[so].astype(jnp.float32)
-    mix_ref[...] = mixed.astype(jnp.bfloat16)
-
-    for copy in pending:
-        copy.wait_send()
+            t2[so, :, cols] = total.astype(jnp.bfloat16)
+            pending.append(
+                send(t2.at[so, :, cols], rz2.at[s, :, cols], pz_s.at[i, h], pz_r.at[s, h], seq=so)
+            )
+        else:
+            last[h] = total
+
+    ahead = 2
+    for at, unit in enumerate(units):
+        if at >= ahead:
+            chips_sum(*units[at - ahead])
+        cores_sum(*unit)
+    for unit in units[len(units) - ahead :]:
+        chips_sum(*unit)
+    for h in range(2):
+        cols = pl.ds(*halves[h])
+        mixed = last[h]
+        for d in range(1, S):
+            so = seq_at(S - d)
+            arrived(rz2.at[so, :, cols], pz_r.at[so, h])
+            mixed = mixed + rz2[so, :, cols].astype(jnp.float32)
+        mix_ref[:, cols] = mixed.astype(jnp.bfloat16)
+
+    for finish in pending:
+        finish()
 
     def drain(k, carry):
-        for d in range(1, S):
-            v_copy(k, d).wait_send()
+        for d in range(S):
+            for here, so, more, target, way in line(d):
+                @pl.when(here & more)
+                def _(so=so, way=way, target=target):
+                    v_copy(k, so, way, target).wait_send()
+
         return carry
 
     lax.fori_loop(0, n, drain, 0)
@@ -359,8 +480,8 @@
     total = packed.shape[0]
     piece = -(-total // (16 * E)) * 16
     packed = jnp.pad(packed, ((0, piece * E - total), (0, 0)))
-    own = lax.dynamic_slice_in_dim(packed, lax.axis_index("expert") * piece, piece, axis=0)
     width = packed.shape[1]
+    own = packed.reshape(E, piece, width)
     bf, f32 = jnp.bfloat16, jnp.float32
     dma, vmem = pltpu.SemaphoreType.DMA, pltpu.VMEM
     in_vmem = pl.BlockSpec(memory_space=pltpu.VMEM)
@@ -376,12 +497,12 @@
         vmem((S, 2, Y, TOK, C), bf), vmem((S, Y, TOK, C), bf), vmem((S, Y, TOK, C), bf),
         vmem((S, Y, TOK, C), bf), vmem((S, TOK, C), bf), vmem((S, TOK, C), bf),
         dma((heads,)), dma((5,)),
-        dma((S,)), dma((S, Y)), dma((S, Y)), dma((S, E)),
+        dma((S, 2)), dma((S, Y)), dma((S, Y)), dma((S, E)),
         dma((E,)), dma((E,)),
-        dma((n, S)), dma((n, S)),
+        dma((n, S, 2)), dma((n, S)),
         dma((Y,)), dma, dma((Y,)),
-        dma((S,)), dma((S, Y)), dma((S, Y)), dma((S, E)),
-        dma((S,)), dma((S,)), dma((S, Y)), dma((S, Y)), dma((S,)), dma((S,)),
+        dma((S, 2)), dma((S, Y)), dma((S, Y)), dma((S, E)),
+        dma((S,)), dma((S,)), dma((S, Y, 2)), dma((S, Y, 2)), dma((S, 2)), dma((S, 2)),
     ]
     return pl.pallas_call(
         functools.partial(layer_kernel, (S, E, G, ctx_dev, tool_dev)),

time: 164 us -> 139 us (0.85)
  Pallas kernels: 153 us -> 126 us
    pallas_call x1, Pallas kernels: 153 us -> 126 us  [on_device(): pl.pallas_call(functools.partial(layer_kernel, (S, E, G, ctx_dev, tool_de...]
    unnamed x5 -> x6, local copies, waits for them, and re-layouts: 6.9 us -> 7.64 us
where the time goes in v2:
time: 139 us; the launch traced here: 138 us
  Pallas kernels  126 us (91%)
  local copies, waits for them, and re-layouts  7.76 us (6%)
  other arithmetic  2.75 us (2%)
    pallas_call x1, Pallas kernels, on_device(): pl.pallas_call(functools.partial(layer_kernel, (S, E, G, ctx_dev, tool_de...  126 us
    unnamed x6, local copies, waits for them, and re-layouts  7.64 us

profile of v2, /device:TPU:0, one launch (start us, length us, event | category | flops | bytes accessed | tf_op | source)
XLA Modules:
  0.0 137.9 jit_solution(5283466061823558174)
XLA Ops:
  1.3 0.8 copy.20
  2.1 0.8 copy.19
  2.9 0.8 pad_maximum_fusion
  3.7 1.4 %copy.23.routes_ref = s32[64,2]{1,0:T(8,128)} copy(s32[64,2]{0,1:T(2,128)} %param.29) | data formatting | bytes 1024 | tf_op args[12]
  5.1 1.4 %copy.24.probs_ref = f32[64,2]{1,0:T(8,128)} copy(f32[64,2]{0,1:T(2,128)} %param.30) | data formatting | bytes 1024 | tf_op args[13]
  6.5 0.1 copy.21
  6.6 1.9 %fusion.8 = bf16[384,640]{1,0:T(8,128)(2,1)} fusion(bf16[352,64]{1,0:T(8,128)(2,1)S(1)} %copy.21, bf16[32,512]{1,0:T(8,128)(2,1)} %param.21, bf16[64,512]{1,0:T(8,128)(2,1)} %param.24, bf16[256,512]{1,0:T(8,128)(2,1)} %param.19), kind=kLoop, calls=%fused_computation.9 | loop fusion | flops 3932160 | bytes 897024 | tf_op jit(solution)/shard_map/concatenate | solution.py:479
  8.5 126.1 %shard_map.176 = (bf16[64,1792]{1,0:T(8,128)(2,1)}, bf16[64,1792]{1,0:T(8,128)(2,1)}) custom-call(s32[1]{0:T(128)S(6)} %copy.27.offset_ref, bf16[4,96,640]{2,1,0:T(8,128)(2,1)} %bitcast.1, bf16[64,2048]{1,0:T(8,128)(2,1)} %qr_ref.1, bf16[64,1792]{1,0:T(8,128)(2,1)} %resid_ref.1, s32[64,2]{1,0:T(8,128)} %copy.23.routes_ref, f32[64,2]{1,0:T(8,128)} %copy.24.probs_ref, ...), custom_call_target="tpu_custom_call" | custom-call | tf_op jit(solution)/shard_map/pallas_call | solution.py:507
  134.7 1.6 %copy.28 = bf16[64,1792]{1,0:T(8,128)(2,1)} copy(bf16[64,1792]{1,0:T(8,128)(2,1)} %get-tuple-element.4) | data formatting | bytes 458752
  136.3 1.6 %copy.29 = bf16[64,1792]{1,0:T(8,128)(2,1)} copy(bf16[64,1792]{1,0:T(8,128)(2,1)} %get-tuple-element.5) | data formatting | bytes 458752

commit v3 on v2

--- a/solution.py
+++ b/solution.py
@@ -28,12 +28,13 @@
 
 def layer_kernel(
     dims,
-    offset_ref, kv_ref, qr_ref, resid_ref, routes_ref, probs_ref,
+    offset_ref, qr_ref, resid_ref, routes_ref, probs_ref,
+    cache_ref, cturn_ref, tool_ref, tturn_ref, suf_ref, sturn_ref,
     q_hbm, wuv_hbm, wout_hbm, wg_hbm, wu_hbm, wd_hbm,
     attn_ref, mix_ref,
     q_buf, wuv, wout, wg, wu, wd,
     kx, tool_buf, keys, wts, allv, oacc,
-    p1, rc1, q1, ry1, xg, p2, rc2, q2, ry2, t2, rz2,
+    p1, rc1, q1, ry1, xg, square_acc, gate_acc, upper_acc, p2, rc2, q2, ry2, t2, rz2,
     q_sem, w_sem,
     kz_s, ky_s, kc_s, k_r,
     wt_s, wt_r,
@@ -108,14 +109,48 @@
             ((wuv_hbm, wuv), (wout_hbm, wout), (wg_hbm.at[0], wg), (wu_hbm.at[0], wu), (wd_hbm.at[0], wd))
         )
     ]
-    kx[s] = kv_ref[...]
+    place = jnp.where(
+        lax.rem(lax.broadcasted_iota(jnp.int32, (rope, lanes), 1), rope)
+        == lax.broadcasted_iota(jnp.int32, (rope, lanes), 0),
+        1.0, 0.0,
+    ).astype(jnp.bfloat16)
+    piece = kx.shape[2]
+    first = 0
+    for latents, turned in (
+        (cache_ref[...], lax.dot_general(
+            cturn_ref[...], place, (((0,), (0,)), ((), ())), preferred_element_type=jnp.float32)),
+        (suf_ref[...], dot(sturn_ref[...], place)),
+        (tool_ref[...], dot(tturn_ref[...], place)),
+        (None, None),
+    ):
+        end = E * piece if latents is None else first + latents.shape[0]
+        at = first
+        while at < end:
+            stop = min(end, (at // piece + 1) * piece)
+            rows = slice(at % piece, at % piece + stop - at)
+            if latents is None:
+                kx[s, at // piece, rows] = jnp.zeros((stop - at, kx.shape[3]), jnp.bfloat16)
+            else:
+                kx[s, at // piece, rows, :LAT] = latents[at - first : stop - first]
+                kx[s, at // piece, rows, LAT:] = turned[at - first : stop - first].astype(jnp.bfloat16)
+            at = stop
+        first = end
     lane_tok = lax.broadcasted_iota(jnp.int32, (TOK, lanes), 1)
-    routes = routes_ref[...]
     probs = probs_ref[...]
-    weight = 2.5 * probs / jnp.sum(probs, axis=1, keepdims=True)
+    weight = 2.5 * probs / jnp.sum(probs, axis=0, keepdims=True)
+    routes = routes_ref[...].astype(jnp.float32)
+    same = lax.broadcasted_iota(jnp.int32, (TOK, TOK), 0) == lax.broadcasted_iota(
+        jnp.int32, (TOK, TOK), 1
+    )
+
+    def upright(row):
+        return jnp.sum(jnp.where(same, row, 0.0), axis=1, keepdims=True)
+
     mine = jnp.zeros((TOK, lanes), jnp.float32)
-    for k in range(routes.shape[1]):
-        mine = mine + jnp.where(routes[:, k : k + 1] == lane_tok, weight[:, k : k + 1], 0.0)
+    for k in range(routes.shape[0]):
+        mine = mine + jnp.where(
+            upright(routes[k : k + 1]) == lane_tok.astype(jnp.float32), upright(weight[k : k + 1]), 0.0
+        )
     wts[e] = mine
 
     pl.semaphore_wait(barrier, S - 1 + E - 1)
@@ -146,7 +181,7 @@
         pending.append(send_when(s + 1 < S, own, own, zs.at[s, 0], rs.at[s, e], seq=s + 1))
         pending.append(send_when(s >= 1, own, own, zs.at[s, 1], rs.at[s, e], seq=s - 1))
 
-    def gather_forward(buf, zs, ys, cs, rs, with_own):
+    def gather_forward(buf, zs, ys, cs, rs, with_own, use):
         def beside(so):
             block = buf.at[so, e]
             for d in range(1, Y):
@@ -160,27 +195,37 @@
                 arrived(block, rs.at[so, eo])
                 send(block, block, cs.at[so, d], rs.at[so, eo], expert=sister)
 
-        if with_own:
-            beside(s)
-        for d in range(1, S):
-            for here, so, more, target, way in line(d):
-                @pl.when(here)
-                def _(so=so, more=more, target=target, way=way):
-                    block = buf.at[so, e]
-                    arrived(block, rs.at[so, e])
-
-                    @pl.when(more)
-                    def _():
-                        send(block, block, zs.at[so, way], rs.at[so, e], seq=target)
-
-                    beside(so)
-        if with_own:
-            onward(s)
-        for d in range(1, S):
-            for here, so, more, target, way in line(d):
-                @pl.when(here)
-                def _(so=so):
-                    onward(so)
+        def over(d, act):
+            if d == 0:
+                if with_own:
+                    act(s, None, None, None)
+            elif 0 < d < S:
+                for here, so, more, target, way in line(d):
+                    @pl.when(here)
+                    def _(so=so, more=more, target=target, way=way):
+                        act(so, more, target, way)
+
+        def relay(so, more, target, way):
+            if more is not None:
+                block = buf.at[so, e]
+                arrived(block, rs.at[so, e])
+
+                @pl.when(more)
+                def _():
+                    send(block, block, zs.at[so, way], rs.at[so, e], seq=target)
+
+            beside(so)
+
+        def complete(so, more, target, way):
+            for d in range(Y):
+                eo = y_at(d) * 2 + 1 - c
+                arrived(buf.at[so, eo], rs.at[so, eo])
+            use(so)
+
+        for d in range(S + 2):
+            over(d, relay)
+            over(d - 1, lambda so, *rest: onward(so))
+            over(d - 2, complete)
 
         def finish():
             def sent(so):
@@ -204,12 +249,6 @@
 
         pending.append(finish)
 
-    def gather_end(buf, rs, i):
-        so = seq_at(i)
-        for d in range(Y):
-            eo = y_at(d) * 2 + 1 - c
-            arrived(buf.at[so, eo], rs.at[so, eo])
-
     gather_start(kx, kz_s, k_r)
     for d in range(1, E):
         pending.append(
@@ -218,9 +257,7 @@
     lax.fori_loop(0, heads, start_q, 0)
     for load in loads:
         load.start()
-    gather_forward(kx, kz_s, ky_s, kc_s, k_r, False)
-    for i in range(1, S):
-        gather_end(kx, k_r, i)
+    gather_forward(kx, kz_s, ky_s, kc_s, k_r, False, lambda so: None)
 
     width = kx.shape[3]
     for so in range(S):
@@ -331,26 +368,42 @@
 
     lax.fori_loop(0, n + lag * (S - 1), turn, 0)
 
-    for yy in range(Y):
-        for cc in range(2):
-            b = yy * 2 + cc
-            p1[cc, yy] = oacc[b * TOK : (b + 1) * TOK].astype(jnp.bfloat16)
-    pending.append(send(p1.at[1 - c], rc1, o_s.at[0], oc_r, expert=sister))
-    arrived(rc1, oc_r)
-    for yy in range(Y):
-        q1[yy] = (p1[c, yy].astype(jnp.float32) + rc1[yy].astype(jnp.float32)).astype(jnp.bfloat16)
-    for d in range(1, Y):
-        yo = y_at(d)
-        pending.append(send(q1.at[yo], ry1.at[y], o_s.at[d], oy_r.at[y], expert=yo * 2 + c))
-    summed = resid_ref[...].astype(jnp.float32) + q1[y].astype(jnp.float32)
-    for d in range(1, Y):
-        yo = y_at(d)
-        arrived(ry1.at[yo], oy_r.at[yo])
-        summed = summed + ry1[yo].astype(jnp.float32)
-    stream = summed.astype(jnp.bfloat16)
-    xg[s, e] = stream
+    cut = C // 256 * 128
+    halves = ((0, cut), (cut, C - cut))
+    for h in range(2):
+        cols = pl.ds(*halves[h])
+        for yy in range(Y):
+            for cc in range(2):
+                b = yy * 2 + cc
+                p1[cc, yy, :, cols] = oacc[b * TOK : (b + 1) * TOK, cols].astype(jnp.bfloat16)
+        pending.append(
+            send(p1.at[1 - c, :, :, cols], rc1.at[:, :, cols], o_s.at[0, h], oc_r.at[h], expert=sister)
+        )
+    for h in range(2):
+        cols = pl.ds(*halves[h])
+        arrived(rc1.at[:, :, cols], oc_r.at[h])
+        for d in range(1, Y + 1):
+            yo = y_at(d)
+            q1[yo, :, cols] = (
+                p1[c, yo, :, cols].astype(jnp.float32) + rc1[yo, :, cols].astype(jnp.float32)
+            ).astype(jnp.bfloat16)
+            if d < Y:
+                pending.append(
+                    send(
+                        q1.at[yo, :, cols], ry1.at[y, :, cols], o_s.at[d, h], oy_r.at[y, h],
+                        expert=yo * 2 + c,
+                    )
+                )
+    for h in range(2):
+        cols = pl.ds(*halves[h])
+        summed = resid_ref[:, cols].astype(jnp.float32) + q1[y, :, cols].astype(jnp.float32)
+        for d in range(1, Y):
+            yo = y_at(d)
+            arrived(ry1.at[yo, :, cols], oy_r.at[yo, h])
+            summed = summed + ry1[yo, :, cols].astype(jnp.float32)
+        xg[s, e, :, cols] = summed.astype(jnp.bfloat16)
     gather_start(xg, xz_s, x_r)
-    attn_ref[...] = stream
+    attn_ref[...] = xg[s, e]
 
     for d in range(1, E):
         eo = lax.rem(e + d, E)
@@ -360,22 +413,22 @@
     own_weight = jnp.sum(
         jnp.where(lane_all == e, wts[...].reshape(rows_all, lanes), 0.0), axis=1, keepdims=True
     )
-    gather_forward(xg, xz_s, xy_s, xc_s, x_r, True)
-
     loads[2].wait()
     loads[3].wait()
-    square = jnp.zeros((rows_all, 1), jnp.float32)
-    gate = jnp.zeros((rows_all, wg.shape[1]), jnp.float32)
-    upper = jnp.zeros((rows_all, wg.shape[1]), jnp.float32)
-    for i in range(S):
-        gather_end(xg, x_r, i)
-        so = seq_at(i)
+    square_acc[...] = jnp.zeros_like(square_acc)
+    gate_acc[...] = jnp.zeros_like(gate_acc)
+    upper_acc[...] = jnp.zeros_like(upper_acc)
+
+    def enter(so):
         x = xg[so].reshape(rows_all, C)
         at = pl.ds(pl.multiple_of(so * C, C), C)
         wide = x.astype(jnp.float32)
-        square = square + jnp.sum(wide * wide, axis=1, keepdims=True)
-        gate = gate + dot(x, wg[at, :])
-        upper = upper + dot(x, wu[at, :])
+        square_acc[...] += jnp.sum(wide * wide, axis=1, keepdims=True)
+        gate_acc[...] += dot(x, wg[at, :])
+        upper_acc[...] += dot(x, wu[at, :])
+
+    gather_forward(xg, xz_s, xy_s, xc_s, x_r, True, enter)
+    square, gate, upper = square_acc[...], gate_acc[...], upper_acc[...]
     inv = lax.rsqrt(square * (1.0 / (S * C)) + norm_eps)
     gate = gate * inv
     inner = (gate / (1.0 + jnp.exp(-gate)) * (upper * inv) * own_weight).astype(jnp.bfloat16)
@@ -390,8 +443,6 @@
                     b = yy * 2 + cc
                     p2[so, cc, yy, :, j : j + tile] = part[b * TOK : (b + 1) * TOK]
         pending.append(send(p2.at[so, 1 - c], rc2.at[so], pc_s.at[i], pc_r.at[so], expert=sister))
-    cut = C // 256 * 128
-    halves = ((0, cut), (cut, C - cut))
     units = [(i, h) for i in range(S) for h in range(2)]
     last = [None, None]
 
@@ -474,14 +525,8 @@
     G = max(g for g in range(1, heads + 1) if heads % g == 0 and g * T <= max(256, 2 * T) and g * rope % lanes == 0)
     n = heads // G
     F = w_gate.shape[2]
-    latents = jnp.concatenate([cache_lat, suf_lat, tool_lat], axis=0)
-    turned = jnp.concatenate([cache_rope, suf_rope, tool_rope], axis=0)
-    packed = jnp.concatenate([latents] + [turned] * (lanes // rope), axis=1)
-    total = packed.shape[0]
-    piece = -(-total // (16 * E)) * 16
-    packed = jnp.pad(packed, ((0, piece * E - total), (0, 0)))
-    width = packed.shape[1]
-    own = packed.reshape(E, piece, width)
+    piece = -(-(ctx_dev + T + tool_dev) // (16 * E)) * 16
+    width = LAT + lanes
     bf, f32 = jnp.bfloat16, jnp.float32
     dma, vmem = pltpu.SemaphoreType.DMA, pltpu.VMEM
     in_vmem = pl.BlockSpec(memory_space=pltpu.VMEM)
@@ -494,26 +539,31 @@
         vmem((n, S, T, G * VD), bf), vmem((S * T, C), f32),
         vmem((2, Y, TOK, C), bf), vmem((Y, TOK, C), bf), vmem((Y, TOK, C), bf), vmem((Y, TOK, C), bf),
         vmem((S, E, TOK, C), bf),
+        vmem((E * TOK, 1), f32), vmem((E * TOK, F), f32), vmem((E * TOK, F), f32),
         vmem((S, 2, Y, TOK, C), bf), vmem((S, Y, TOK, C), bf), vmem((S, Y, TOK, C), bf),
         vmem((S, Y, TOK, C), bf), vmem((S, TOK, C), bf), vmem((S, TOK, C), bf),
         dma((heads,)), dma((5,)),
         dma((S, 2)), dma((S, Y)), dma((S, Y)), dma((S, E)),
         dma((E,)), dma((E,)),
         dma((n, S, 2)), dma((n, S)),
-        dma((Y,)), dma, dma((Y,)),
+        dma((Y, 2)), dma((2,)), dma((Y, 2)),
         dma((S, 2)), dma((S, Y)), dma((S, Y)), dma((S, E)),
         dma((S,)), dma((S,)), dma((S, Y, 2)), dma((S, Y, 2)), dma((S, 2)), dma((S, 2)),
     ]
     return pl.pallas_call(
         functools.partial(layer_kernel, (S, E, G, ctx_dev, tool_dev)),
         out_shape=(jax.ShapeDtypeStruct((TOK, C), bf), jax.ShapeDtypeStruct((TOK, C), bf)),
-        in_specs=[pl.BlockSpec(memory_space=pltpu.SMEM)] + [in_vmem] * 5 + [anywhere] * 6,
+        in_specs=[pl.BlockSpec(memory_space=pltpu.SMEM)] + [in_vmem] * 10 + [anywhere] * 6,
         out_specs=(in_vmem, in_vmem),
         scratch_shapes=scratch,
         compiler_params=pltpu.CompilerParams(
             collective_id=0, has_side_effects=True, vmem_limit_bytes=61 * 1024 * 1024
         ),
-    )(offset, own, q_rope, resid, routes, probs, q_lat, w_uv, w_out, w_gate, w_up, w_down)
+    )(
+        offset, q_rope, resid, routes.T, probs.T,
+        cache_lat, cache_rope.T, tool_lat, tool_rope, suf_lat, suf_rope,
+        q_lat, w_uv, w_out, w_gate, w_up, w_down,
+    )
 
 
 def solution(mesh):

time: 139 us -> 131 us (0.942)
  local copies, waits for them, and re-layouts: 7.76 us -> 3.28 us
  other arithmetic: 2.75 us -> 0 us
    unnamed x6 -> x2, local copies, waits for them, and re-layouts: 7.64 us -> 3.28 us
    concatenate x2 -> x0, other arithmetic: 2.75 us -> none  [the longest x1 1.9 us: on_device(): packed = jnp.concatenate([latents] + [turned] * (lanes // rope), axis=1)]
where the time goes in v3:
time: 131 us
  Pallas kernels  126 us (96%)
  local copies, waits for them, and re-layouts  3.28 us (3%)
    pallas_call x1, Pallas kernels, on_device(): pl.pallas_call(functools.partial(layer_kernel, (S, E, G, ctx_dev, tool_de...  126 us
    unnamed x2, local copies, waits for them, and re-layouts  3.28 us

profile of v3, /device:TPU:0, one launch (start us, length us, event | category | flops | bytes accessed | tf_op | source)
XLA Modules:
  0.0 130.8 jit_solution(9995379527780805502)
XLA Ops:
  1.3 126.2 %shard_map.176 = (bf16[64,1792]{1,0:T(8,128)(2,1)}, bf16[64,1792]{1,0:T(8,128)(2,1)}) custom-call(s32[1]{0:T(128)S(6)} %copy.21.offset_ref, bf16[64,2048]{1,0:T(8,128)(2,1)} %qr_ref.1, bf16[64,1792]{1,0:T(8,128)(2,1)} %resid_ref.1, s32[2,64]{1,0:T(2,128)} %bitcast.4, f32[2,64]{1,0:T(2,128)} %bitcast.5, bf16[256,512]{1,0:T(8,128)(2,1)} %cache_ref.1, ...), custom_call_target="tpu_custom_call" | custom-call | tf_op jit(solution)/shard_map/pallas_call | solution.py:553
  127.5 1.6 %copy.22 = bf16[64,1792]{1,0:T(8,128)(2,1)} copy(bf16[64,1792]{1,0:T(8,128)(2,1)} %get-tuple-element.4) | data formatting | bytes 458752
  129.1 1.6 %copy.23 = bf16[64,1792]{1,0:T(8,128)(2,1)} copy(bf16[64,1792]{1,0:T(8,128)(2,1)} %get-tuple-element.5) | data formatting | bytes 458752

commit v4 on v3

--- a/solution.py
+++ b/solution.py
@@ -340,10 +340,6 @@
     lag = 2
 
     def turn(k, carry):
-        @pl.when(k < n)
-        def _():
-            attend(k)
-
         for d in range(1, S):
             at = k - lag * d
 
@@ -357,6 +353,10 @@
                         @pl.when(more)
                         def _():
                             v_copy(at, so, way, target).start()
+
+        @pl.when(k < n)
+        def _():
+            attend(k)
 
         done = k - lag * (S - 1)
 
@@ -434,7 +434,8 @@
     inner = (gate / (1.0 + jnp.exp(-gate)) * (upper * inv) * own_weight).astype(jnp.bfloat16)
 
     loads[4].wait()
-    for i in range(S):
+
+    def produce(i):
         so = seq_at(i + 1)
         for j in range(0, C, tile):
             part = dot(inner, wd[:, pl.ds(pl.multiple_of(so * C + j, 128), tile)]).astype(jnp.bfloat16)
@@ -481,7 +482,10 @@
             last[h] = total
 
     ahead = 2
+    produce(0)
     for at, unit in enumerate(units):
+        if unit[1] == 0 and unit[0] + 1 < S:
+            produce(unit[0] + 1)
         if at >= ahead:
             chips_sum(*units[at - ahead])
         cores_sum(*unit)

time: 131 us -> 132 us (level)
  no operation moved by 1% of the time
where the time goes in v4:
time: 132 us
  Pallas kernels  127 us (96%)
  local copies, waits for them, and re-layouts  3.28 us (2%)
    pallas_call x1, Pallas kernels, on_device(): pl.pallas_call(functools.partial(layer_kernel, (S, E, G, ctx_dev, tool_de...  127 us
    unnamed x2, local copies, waits for them, and re-layouts  3.28 us

profile of v4, /device:TPU:0, one launch (start us, length us, event | category | flops | bytes accessed | tf_op | source)
XLA Modules:
  0.0 131.7 jit_solution(16470471760244204392)
XLA Ops:
  1.3 127.1 %shard_map.176 = (bf16[64,1792]{1,0:T(8,128)(2,1)}, bf16[64,1792]{1,0:T(8,128)(2,1)}) custom-call(s32[1]{0:T(128)S(6)} %copy.21.offset_ref, bf16[64,2048]{1,0:T(8,128)(2,1)} %qr_ref.1, bf16[64,1792]{1,0:T(8,128)(2,1)} %resid_ref.1, s32[2,64]{1,0:T(2,128)} %bitcast.4, f32[2,64]{1,0:T(2,128)} %bitcast.5, bf16[256,512]{1,0:T(8,128)(2,1)} %cache_ref.1, ...), custom_call_target="tpu_custom_call" | custom-call | tf_op jit(solution)/shard_map/pallas_call | solution.py:557
  128.4 1.6 %copy.22 = bf16[64,1792]{1,0:T(8,128)(2,1)} copy(bf16[64,1792]{1,0:T(8,128)(2,1)} %get-tuple-element.4) | data formatting | bytes 458752
  130.0 1.6 %copy.23 = bf16[64,1792]{1,0:T(8,128)(2,1)} copy(bf16[64,1792]{1,0:T(8,128)(2,1)} %get-tuple-element.5) | data formatting | bytes 458752
